TPU v7x, 256 devices: a whole 4x4x8 slice. The times are simulated.
256 devices in a mesh: loop: 32 (over x_hi, z, core), tensor: 8 (over y, x_lo).
Axes of the slice: x: 4 (x_hi: 2, x_lo: 2; x = x_hi * 2 + x_lo), y: 4, z: 8, core: 2. Of those that a mesh axis runs over, the one named last changes fastest.
Arguments:
- context: bfloat16 [10240, 5120], P('loop', 'tensor'), may hold values from -6 to 6
- w_out: bfloat16 [5120, 5120], P('tensor', 'loop'), may hold values from -0.078125 to 0.078125
- residual: bfloat16 [10240, 5120], P('loop', 'tensor'), may hold values from -70 to 70
- gain: float32 [5120], replicated, may hold values from 0.1 to 1.9
- grad_out: bfloat16 [10240, 5120], P('loop', 'tensor'), may hold values from -6 to 6
Outputs:
- normed: bfloat16 [10240, 5120], P('loop', 'tensor')
- d_context: bfloat16 [10240, 5120], P('loop', 'tensor')
- w_grad: float32 [5120, 5120], P('loop', 'tensor')
All inputs are finite; a program needn't handle non-finite values.
Results may differ from a plain program's by a relative error of at most 0.0049.
Values may be sent and summed in bfloat16 or wider, within the bound.
No kernel may reach another device: no remote copies, remote signals or barrier semaphores. Data moves between devices by JAX's collectives and lax.ppermute only.
A program may use at most 128 MiB of HBM per device.

v0:
```python
import math
import jax
import jax.numpy as jnp
from jax import lax
from jax.sharding import PartitionSpec as P

D = 5120


def per_device(context, w_out, residual, gain, grad_out):
    slot = lax.axis_index("tensor")
    local = residual.shape[1]
    width = D
    partial_value = jnp.dot(
        context,
        lax.all_gather(w_out, "loop", axis=1, tiled=True),
        preferred_element_type=jnp.float32,
    )
    hidden = lax.psum_scatter(
        partial_value, "tensor", scatter_dimension=1, tiled=True
    ) + residual.astype(jnp.float32)
    own_gain = lax.dynamic_slice_in_dim(gain, slot * local, local, 0)
    scaled = own_gain[None, :] * grad_out.astype(jnp.float32)
    square_sum, cross_sum = lax.psum(
        (jnp.sum(hidden * hidden, axis=1), jnp.sum(hidden * scaled, axis=1)), "tensor"
    )
    root = lax.rsqrt(square_sum / width + 1e-06)[:, None]
    dot = (cross_sum / width)[:, None]
    normed = (hidden * root * own_gain[None, :]).astype(jnp.bfloat16)
    own_grad = (root * scaled - hidden * root * root * root * dot).astype(jnp.bfloat16)
    d_hidden = lax.all_gather(own_grad, "tensor", axis=1, tiled=True)
    columns = d_hidden
    d_sum = lax.dot_general(
        columns,
        lax.all_gather(w_out, "loop", axis=1, tiled=True),
        (((1,), (1,)), ((), ())),
        preferred_element_type=jnp.float32,
    )
    d_context = d_sum.astype(jnp.bfloat16)
    factor = 1.0 / math.sqrt(context.shape[0] * lax.axis_size("loop"))
    columns = d_hidden
    w_grad = lax.psum_scatter(
        lax.dot_general(
            columns, context, (((0,), (0,)), ((), ())), preferred_element_type=jnp.float32
        )
        * factor,
        "loop",
        scatter_dimension=0,
        tiled=True,
    )
    return (normed, d_context, w_grad)


def solution(mesh):
    return jax.shard_map(
        per_device,
        mesh=mesh,
        in_specs=(
            P("loop", "tensor"),
            P("tensor", "loop"),
            P("loop", "tensor"),
            P(),
            P("loop", "tensor"),
        ),
        out_specs=(P("loop", "tensor"), P("loop", "tensor"), P("loop", "tensor")),
        check_vma=False,
    )
```

profile of v0, /device:TPU:8, one launch (start us, length us, event | category | flops | bytes accessed | tf_op | source)
XLA Modules:
  0.0 542.7 jit_solution(374131623523673046)
XLA Ops:
  7.2 0.0 copy-start
  7.2 0.0 all-gather.3.cloned.1.call-start
  7.2 0.7 all-gather.3.cloned.1.call-update
  7.9 0.0 reduce-scatter.3.cloned.1.call-start
  8.0 100.9 %all-gather.3.cloned.1.call-done = bf16[640,5120]{0,1:T(8,128)(2,1)} async-done(((bf16[640,160]{0,1:T(8,128)(2,1)}), bf16[640,5120]{0,1:T(8,128)(2,1)}) %all-gather.3.cloned.1.call-update) | async-done | bytes 6553616 | tf_op jit(solution)/shard_map/all_gather | solution.py:16
  108.8 0.0 copy-done
  108.8 9.2 %fusion = f32[320,5120]{1,0:T(8,128)} fusion(bf16[320,640]{1,0:T(8,128)(2,1)S(1)} %copy-done, bf16[640,5120]{0,1:T(8,128)(2,1)} %all-gather.3.cloned.1.call-done), kind=kOutput, calls=%fused_computation.10 | convolution fusion | flops 2097152000 | bytes 13516800 | tf_op jit(solution)/shard_map/dot_general | solution.py:14
  118.0 0.0 copy-start.1
  118.0 0.0 copy-start.2
  118.0 0.0 reduce-scatter.3.cloned.1.call-update
  118.1 0.0 all-gather.5.cloned.1.call-start
  118.1 0.8 dynamic_slice.3
  119.0 133.1 %reduce-scatter.3.cloned.1.call-done = f32[320,640]{1,0:T(8,128)} async-done(((f32[320,5120]{1,0:T(8,128)}), f32[320,640]{1,0:T(8,128)}) %reduce-scatter.3.cloned.1.call-update) | async-done | bytes 819216 | tf_op jit(solution)/shard_map/reduce_scatter | solution.py:19
  252.0 0.0 copy-done.1
  252.0 0.0 copy-done.2
  252.0 1.4 multiply_reduce_fusion
  253.5 16.3 %all-reduce = (f32[320]{0:T(512)S(1)}, f32[320]{0:T(512)S(1)}) all-reduce(f32[320]{0:T(512)S(1)} %get-tuple-element.4, f32[320]{0:T(512)S(1)} %get-tuple-element.3), channel_id=1, replica_groups=mesh['loop'=32,'tensor'=8] {'tensor'}, use_global_device_ids=true, to_apply=%region_2.0 | all-reduce | flops 640 | bytes 5120 | tf_op jit(solution)/shard_map/psum | solution.py:24
  269.8 2.4 subtract_convert_fusion
  272.2 0.0 all-gather.5.cloned.1.call-update
  272.2 0.0 reduce-scatter.5.cloned.1.call-start
  272.2 76.4 %all-gather.5.cloned.1.call-done = bf16[320,5120]{1,0:T(8,128)(2,1)} async-done(((bf16[320,640]{1,0:T(8,128)(2,1)}), bf16[320,5120]{1,0:T(8,128)(2,1)}) %all-gather.5.cloned.1.call-update) | async-done | bytes 3276816 | tf_op jit(solution)/shard_map/all_gather | solution.py:31
  348.6 10.6 %convolution_multiply_fusion = f32[5120,640]{1,0:T(8,128)} fusion(bf16[320,5120]{1,0:T(8,128)(2,1)} %all-gather.5.cloned.1.call-done, bf16[320,640]{1,0:T(8,128)(2,1)S(1)} %copy-done), kind=kOutput, calls=%fused_computation | convolution fusion | flops 2100428800 | bytes 16793600 | tf_op jit(solution)/shard_map/dot_general | solution.py:43
  359.2 0.0 reduce-scatter.5.cloned.1.call-update
  359.2 7.3 %convolution_convert_fusion = bf16[320,640]{1,0:T(8,128)(2,1)} fusion(bf16[320,5120]{1,0:T(8,128)(2,1)} %all-gather.5.cloned.1.call-done, bf16[640,5120]{0,1:T(8,128)(2,1)} %all-gather.3.cloned.1.call-done), kind=kOutput, calls=%fused_computation.1 | convolution fusion | flops 2097356800 | bytes 10240000 | tf_op jit(solution)/shard_map/dot_general | solution.py:33
  366.5 169.6 %reduce-scatter.5.cloned.1.call-done = f32[160,640]{1,0:T(8,128)} async-done(((f32[5120,640]{1,0:T(8,128)}), f32[160,640]{1,0:T(8,128)}) %reduce-scatter.5.cloned.1.call-update) | async-done | bytes 409616 | tf_op jit(solution)/shard_map/reduce_scatter | solution.py:42
  (1 shorter events, 0.0 us)
Async XLA Ops:
  7.2 101.7 %copy-start = (bf16[320,640]{1,0:T(8,128)(2,1)S(1)}, bf16[320,640]{1,0:T(8,128)(2,1)}, u32[]{:S(2)}) copy-start(bf16[320,640]{1,0:T(8,128)(2,1)} %param.5) | copy-start | bytes 1228804
  7.2 101.6 %all-gather.3.cloned.1.call-start = ((), (), s32[]{:S(2)}) async-start(), calls=%async_computation.2 | async-start | bytes 6758400 | tf_op jit(solution)/shard_map/all_gather | solution.py:16
  7.9 244.1 %reduce-scatter.3.cloned.1.call-start = ((), (), s32[]{:S(2)}) async-start(), calls=%async_computation.3 | async-start | bytes 7372800 | tf_op jit(solution)/shard_map/reduce_scatter | solution.py:19
  118.0 134.0 %copy-start.1 = (bf16[320,640]{1,0:T(8,128)(2,1)S(1)}, bf16[320,640]{1,0:T(8,128)(2,1)}, u32[]{:S(2)}) copy-start(bf16[320,640]{1,0:T(8,128)(2,1)} %param.9) | copy-start | bytes 1228804
  118.0 134.0 %copy-start.2 = (bf16[320,640]{1,0:T(8,128)(2,1)S(1)}, bf16[320,640]{1,0:T(8,128)(2,1)}, u32[]{:S(2)}) copy-start(bf16[320,640]{1,0:T(8,128)(2,1)} %param.7) | copy-start | bytes 1228804
  118.1 230.6 %all-gather.5.cloned.1.call-start = ((), (), s32[]{:S(2)}) async-start(), calls=%async_computation.4 | async-start | bytes 3686400 | tf_op jit(solution)/shard_map/all_gather | solution.py:31
  272.2 264.0 %reduce-scatter.5.cloned.1.call-start = ((), (), s32[]{:S(2)}) async-start(), calls=%async_computation.5 | async-start | bytes 13516800 | tf_op jit(solution)/shard_map/reduce_scatter | solution.py:42
Sparse Core Ops, SparseCore 0:
  10.8 97.9 all-gather.2
  118.2 133.7 reduce-scatter.2
  272.3 76.2 all-gather.4
  359.4 176.7 reduce-scatter.4
where the time goes:
time: 543 us
  waiting for transfers between devices  481 us (89%)
  matrix products  27.1 us (5%)
  blocking collectives  16.3 us (3%)
  between operations  13.8 us (3%)
    reduce_scatter x1, waiting for transfers between devices, per_device(): lax.psum_scatter(lax.dot_general(columns, context, (((0,), (0,)), ((), ()...  170 us
    reduce_scatter x1, waiting for transfers between devices, per_device(): lax.psum_scatter(partial_value, 'tensor', scatter_dimension=1, tiled=True)  133 us
    all_gather x1, waiting for transfers between devices, per_device(): lax.all_gather(w_out, 'loop', axis=1, tiled=True)  101 us
    all_gather x1, waiting for transfers between devices, per_device(): d_hidden = lax.all_gather(own_grad, 'tensor', axis=1, tiled=True)  76.4 us
    psum x1, blocking collectives, per_device(): lax.psum((jnp.sum(hidden * hidden, axis=1), jnp.sum(hidden * scaled, axis...  16.3 us
  transfers between devices with their start and end apart: 4, of which 4 were waited for; matrix products, arithmetic and copies ran while one was open for 2% of the time, Pallas kernels for 0%

commit v1 on v0

--- a/solution.py
+++ b/solution.py
@@ -28,7 +28,10 @@
     dot = (cross_sum / width)[:, None]
     normed = (hidden * root * own_gain[None, :]).astype(jnp.bfloat16)
     own_grad = (root * scaled - hidden * root * root * root * dot).astype(jnp.bfloat16)
-    d_hidden = lax.all_gather(own_grad, "tensor", axis=1, tiled=True)
+    count = lax.axis_size("tensor")
+    blocks = jnp.stack([own_grad for _ in range(count)])
+    blocks = lax.all_to_all(blocks, "tensor", split_axis=0, concat_axis=0)
+    d_hidden = jnp.concatenate(blocks, axis=1)
     columns = d_hidden
     d_sum = lax.dot_general(
         columns,

time: 543 us -> 505 us (0.930)
  waiting for transfers between devices: 481 us -> 404 us
  blocking collectives: 16.3 us -> 55.9 us
    all_gather x1 -> x0, waiting for transfers between devices: 76.4 us -> none  [per_device(): d_hidden = lax.all_gather(own_grad, 'tensor', axis=1, tiled=True)]
    all_to_all x0 -> x1, blocking collectives: none -> 39.6 us  [per_device(): blocks = lax.all_to_all(blocks, 'tensor', split_axis=0, concat_axis=0)]
  transfers between devices with their start and end apart: 4 -> 3, of which waited for: 4 -> 3; matrix products, arithmetic and copies ran while one was open for 2% -> 2% of each run, Pallas kernels for 0% -> 0%
where the time goes in v1:
time: 505 us
  waiting for transfers between devices  404 us (80%)
  blocking collectives  55.9 us (11%)
  matrix products  23.4 us (5%)
  between operations  13.8 us (3%)
    reduce_scatter x1, waiting for transfers between devices, per_device(): lax.psum_scatter(lax.dot_general(columns, context, (((0,), (0,)), ((), ()...  170 us
    reduce_scatter x1, waiting for transfers between devices, per_device(): lax.psum_scatter(partial_value, 'tensor', scatter_dimension=1, tiled=True)  133 us
    all_gather x1, waiting for transfers between devices, per_device(): lax.all_gather(w_out, 'loop', axis=1, tiled=True)  101 us
    all_to_all x1, blocking collectives, per_device(): blocks = lax.all_to_all(blocks, 'tensor', split_axis=0, concat_axis=0)  39.6 us
    psum x1, blocking collectives, per_device(): lax.psum((jnp.sum(hidden * hidden, axis=1), jnp.sum(hidden * scaled, axis...  16.3 us
  transfers between devices with their start and end apart: 3, of which 3 were waited for; matrix products, arithmetic and copies ran while one was open for 2% of the time, Pallas kernels for 0%

profile of v1, /device:TPU:8, one launch (start us, length us, event | category | flops | bytes accessed | tf_op | source)
XLA Modules:
  0.0 504.7 jit_solution(11909428896425616147)
XLA Ops:
  7.2 0.0 copy-start
  7.2 0.0 all-gather.2.cloned.1.call-start
  7.2 0.7 all-gather.2.cloned.1.call-update
  7.9 0.0 reduce-scatter.3.cloned.1.call-start
  8.0 100.9 %all-gather.2.cloned.1.call-done = bf16[640,5120]{0,1:T(8,128)(2,1)} async-done(((bf16[640,160]{0,1:T(8,128)(2,1)}), bf16[640,5120]{0,1:T(8,128)(2,1)}) %all-gather.2.cloned.1.call-update) | async-done | bytes 6553616 | tf_op jit(solution)/shard_map/all_gather | solution.py:16
  108.8 0.0 copy-done
  108.8 9.2 %fusion = f32[320,5120]{1,0:T(8,128)} fusion(bf16[320,640]{1,0:T(8,128)(2,1)S(1)} %copy-done, bf16[640,5120]{0,1:T(8,128)(2,1)} %all-gather.2.cloned.1.call-done), kind=kOutput, calls=%fused_computation.10 | convolution fusion | flops 2097152000 | bytes 13516800 | tf_op jit(solution)/shard_map/dot_general | solution.py:14
  118.0 0.0 copy-start.2
  118.0 0.0 copy-start.3
  118.0 0.0 reduce-scatter.3.cloned.1.call-update
  118.1 0.0 reduce-scatter.5.cloned.1.call-start
  118.1 0.8 dynamic_slice.3
  118.9 133.1 %reduce-scatter.3.cloned.1.call-done = f32[320,640]{1,0:T(8,128)} async-done(((f32[320,5120]{1,0:T(8,128)}), f32[320,640]{1,0:T(8,128)}) %reduce-scatter.3.cloned.1.call-update) | async-done | bytes 819216 | tf_op jit(solution)/shard_map/reduce_scatter | solution.py:19
  252.0 0.0 copy-done.2
  252.0 0.0 copy-done.3
  252.0 1.4 multiply_reduce_fusion
  253.5 16.3 %all-reduce = (f32[320]{0:T(512)S(1)}, f32[320]{0:T(512)S(1)}) all-reduce(f32[320]{0:T(512)S(1)} %get-tuple-element.4, f32[320]{0:T(512)S(1)} %get-tuple-element.3), channel_id=1, replica_groups=mesh['loop'=32,'tensor'=8] {'tensor'}, use_global_device_ids=true, to_apply=%region_2.0 | all-reduce | flops 640 | bytes 5120 | tf_op jit(solution)/shard_map/psum | solution.py:24
  269.8 2.3 subtract_convert_fusion
  272.0 0.3 stack.2
  272.3 39.6 %all_to_all.5 = bf16[8,320,640]{2,1,0:T(8,128)(2,1)S(1)} all-to-all(bf16[8,320,640]{2,1,0:T(8,128)(2,1)S(1)} %stack.2), channel_id=1, replica_groups=mesh['loop'=32,'tensor'=8] {'tensor'}, dimensions={0} | all-to-all | bytes 6553600 | tf_op jit(solution)/shard_map/all_to_all | solution.py:33
  311.9 0.5 copy.9
  312.4 0.0 copy-start.1
  312.4 1.7 copy-done.1
  314.1 6.9 %convolution_multiply_fusion = f32[5120,640]{1,0:T(8,128)} fusion(bf16[320,5120]{1,0:T(8,128)(2,1)S(1)} %bitcast.9, bf16[320,640]{1,0:T(8,128)(2,1)S(1)} %copy-done), kind=kOutput, calls=%fused_computation | convolution fusion | flops 2100428800 | bytes 16793600 | tf_op jit(solution)/shard_map/dot_general | solution.py:46
  321.1 0.0 reduce-scatter.5.cloned.1.call-update
  321.1 7.3 %convolution_convert_fusion = bf16[320,640]{1,0:T(8,128)(2,1)} fusion(bf16[320,5120]{1,0:T(8,128)(2,1)} %bitcast.10, bf16[640,5120]{0,1:T(8,128)(2,1)} %all-gather.2.cloned.1.call-done), kind=kOutput, calls=%fused_computation.1 | convolution fusion | flops 2097356800 | bytes 10240000 | tf_op jit(solution)/shard_map/dot_general | solution.py:36
  328.4 169.8 %reduce-scatter.5.cloned.1.call-done = f32[160,640]{1,0:T(8,128)} async-done(((f32[5120,640]{1,0:T(8,128)}), f32[160,640]{1,0:T(8,128)}) %reduce-scatter.5.cloned.1.call-update) | async-done | bytes 409616 | tf_op jit(solution)/shard_map/reduce_scatter | solution.py:45
  (1 shorter events, 0.0 us)
Async XLA Ops:
  7.2 101.7 %copy-start = (bf16[320,640]{1,0:T(8,128)(2,1)S(1)}, bf16[320,640]{1,0:T(8,128)(2,1)}, u32[]{:S(2)}) copy-start(bf16[320,640]{1,0:T(8,128)(2,1)} %param.5) | copy-start | bytes 1228804
  7.2 101.6 %all-gather.2.cloned.1.call-start = ((), (), s32[]{:S(2)}) async-start(), calls=%async_computation.3 | async-start | bytes 6758400 | tf_op jit(solution)/shard_map/all_gather | solution.py:16
  7.9 244.1 %reduce-scatter.3.cloned.1.call-start = ((), (), s32[]{:S(2)}) async-start(), calls=%async_computation.4 | async-start | bytes 7372800 | tf_op jit(solution)/shard_map/reduce_scatter | solution.py:19
  118.0 134.0 %copy-start.2 = (bf16[320,640]{1,0:T(8,128)(2,1)S(1)}, bf16[320,640]{1,0:T(8,128)(2,1)}, u32[]{:S(2)}) copy-start(bf16[320,640]{1,0:T(8,128)(2,1)} %param.9) | copy-start | bytes 1228804
  118.0 134.0 %copy-start.3 = (bf16[320,640]{1,0:T(8,128)(2,1)S(1)}, bf16[320,640]{1,0:T(8,128)(2,1)}, u32[]{:S(2)}) copy-start(bf16[320,640]{1,0:T(8,128)(2,1)} %param.7) | copy-start | bytes 1228804
  118.1 380.2 %reduce-scatter.5.cloned.1.call-start = ((), (), s32[]{:S(2)}) async-start(), calls=%async_computation.5 | async-start | bytes 13516800 | tf_op jit(solution)/shard_map/reduce_scatter | solution.py:45
  312.4 1.8 copy-start.1
Sparse Core Ops, SparseCore 0:
  10.8 97.9 all-gather.1
  118.2 133.7 reduce-scatter.2
  321.2 176.9 reduce-scatter.4
